TPU v7x, 512 devices: a whole 4x4x16 slice. The times are simulated.
512 devices in a mesh: mesh: 32 (over z, core), run: 16 (over y, x).
Axes of the slice: x: 4, y: 4, z: 16, core: 2. Of those that a mesh axis runs over, the one named last changes fastest.
Arguments:
- snapshots: bfloat16 [65536, 2048], P('mesh', 'run'), may hold values from -6 to 6
- block_cols: int32 [1024, 16], P('mesh'), may hold values from 0 to 1023, as said below
- mass_blocks: bfloat16 [1024, 64, 1024], P('mesh'), as said below
Outputs:
- gram: float32 [2048, 2048], P('mesh', 'run')
Inputs may be any that keep to these rules, and one draw needn't show every extreme that they name: `block_cols`: block row b names 16 different block columns, the first of them b itself; all lie from 2 blocks before the first block row of shard b // 32 to 2 blocks after its last. In every shard but the first, its first block row names the block 2 before the shard; in every shard but the last, its last block row names the block 2 after it. `mass_blocks`: entry [b, i, k * 64 + j] is row i, column j of the k-th stored block of block row b, in the order of block_cols.
All inputs are finite; a program needn't handle non-finite values.
Results may differ from a plain program's by a relative error of at most 0.00056.
Values may be sent and summed in bfloat16 or wider, within the bound.
A program may use at most 64 MiB of HBM per device.

v0:
```python
import jax
import jax.numpy as jnp
from jax import lax
from jax.sharding import PartitionSpec as P

BLK = 64
HB = 2


def extended(block, sides, width):
    for axis, dim in sides:
        count = lax.axis_size(axis)
        forward = [(i, i + 1) for i in range(count - 1)]
        backward = [(target, source) for source, target in forward]
        low = lax.ppermute(
            lax.slice_in_dim(block, block.shape[dim] - width, None, axis=dim), axis, forward
        )
        high = lax.ppermute(lax.slice_in_dim(block, 0, width, axis=dim), axis, backward)
        block = jnp.concatenate([low, block, high], axis=dim)
    return block


def contract_nodes(left_cols, right_cols):
    return lax.dot_general(
        left_cols, right_cols, (((0,), (0,)), ((), ())), preferred_element_type=jnp.float32
    )


def on_device(snapshots, block_cols, mass_blocks):
    node_count = snapshots.shape[0]
    column_count = snapshots.shape[1]
    blocks_here = node_count // BLK
    stored_count = block_cols.shape[1]
    rim_width = HB * BLK
    padded = extended(snapshots, (("mesh", 0),), rim_width)
    shard_index = lax.axis_index("mesh")
    local_cols = block_cols - (shard_index * blocks_here - HB)
    blocked = padded.reshape(blocks_here + 2 * HB, BLK, column_count)
    picked = blocked[local_cols].reshape(blocks_here, stored_count * BLK, column_count)
    weighted = jnp.einsum("bim,bmc->bic", mass_blocks, picked, preferred_element_type=jnp.float32)
    weighted = weighted.astype(jnp.bfloat16).reshape(node_count, column_count)
    gathered = lax.all_gather(snapshots, "run", axis=1, tiled=True)
    partial_term = contract_nodes(gathered, weighted)
    gram = lax.psum_scatter(partial_term, "mesh", scatter_dimension=0, tiled=True)
    return gram


def solution(mesh):
    placed = (P("mesh", "run"), P("mesh", None), P("mesh", None, None))
    return jax.shard_map(
        on_device, mesh=mesh, in_specs=placed, out_specs=P("mesh", "run"), check_vma=False
    )
```

profile of v0, /device:TPU:2, one launch (start us, length us, event | category | flops | bytes accessed | tf_op | source)
XLA Modules:
  0.0 229.1 jit_solution(6387576160055392372)
XLA Ops:
  6.5 0.0 all-gather.2.cloned.1.call-start
  6.5 0.7 all-gather.2.cloned.1.call-update
  7.3 0.0 reduce-scatter.4.cloned.1.call-start
  7.3 0.8 fusion
  8.1 1.7 collective-permute-start
  9.8 1.3 collective-permute-start.1
  11.1 0.7 compare_select_fusion
  11.8 0.1 copy.7
  11.9 0.1 reshape.14
  12.0 0.0 collective-permute-done
  12.0 2.6 %collective-permute-done.1 = bf16[128,128]{1,0:T(8,128)(2,1)S(1)} collective-permute-done((bf16[128,128]{1,0:T(8,128)(2,1)S(1)}, bf16[128,128]{1,0:T(8,128)(2,1)S(1)}, u32[]{:S(2)}, u32[]{:S(2)}) %collective-permute-start.1) | collective-permute-done | bytes 32800 | tf_op jit(solution)/shard_map/ppermute | solution.py:18
  14.6 1.1 pad_maximum_fusion
  15.7 13.4 %gather_fusion = bf16[512,64,128]{2,1,0:T(8,128)(2,1)} fusion(bf16[36,64,128]{2,1,0:T(8,128)(2,1)S(1)} %bitcast.12, s32[1024]{0:T(1024)S(1)} %pad_clamp_fusion), kind=kCustom, calls=%fused_computation | custom fusion | bytes 16779264 | tf_op jit(solution)/shard_map/gather | solution.py:39
  29.1 6.6 %convolution_convert_fusion = bf16[32,128,64]{1,2,0:T(8,128)(2,1)S(1)} fusion(bf16[32,64,1024]{2,1,0:T(8,128)(2,1)} %param.5, bf16[32,1024,128]{2,1,0:T(8,128)(2,1)} %bitcast.13), kind=kOutput, calls=%fused_computation.2 | convolution fusion | flops 537133056 | bytes 13107200 | tf_op jit(solution)/shard_map/bim,bmc->bic/dot_general | solution.py:40
  35.8 72.4 %all-gather.2.cloned.1.call-done = bf16[2048,2048]{1,0:T(8,128)(2,1)} async-done(((bf16[2048,128]{1,0:T(8,128)(2,1)}), bf16[2048,2048]{1,0:T(8,128)(2,1)}) %all-gather.2.cloned.1.call-update) | async-done | bytes 8388624 | tf_op jit(solution)/shard_map/all_gather | solution.py:42
  108.2 4.7 %convolution_bitcast_fusion = f32[2048,128]{0,1:T(8,128)S(1)} fusion(bf16[2048,128]{1,0:T(8,128)(2,1)S(1)} %bitcast.14, bf16[2048,2048]{1,0:T(8,128)(2,1)} %all-gather.2.cloned.1.call-done), kind=kOutput, calls=%fused_computation.1 | convolution fusion | flops 1073741824 | bytes 9961472 | tf_op jit(solution)/shard_map/dot_general | solution.py:24
  112.9 1.3 copy.9
  114.2 0.0 reduce-scatter.4.cloned.1.call-update
  114.2 108.1 %reduce-scatter.4.cloned.1.call-done = f32[64,128]{1,0:T(8,128)} async-done(((f32[2048,128]{1,0:T(8,128)}), f32[64,128]{1,0:T(8,128)}) %reduce-scatter.4.cloned.1.call-update) | async-done | bytes 32784 | tf_op jit(solution)/shard_map/reduce_scatter | solution.py:44
  (1 shorter events, 0.0 us)
Async XLA Ops:
  6.5 101.7 %all-gather.2.cloned.1.call-start = ((), (), s32[]{:S(2)}) async-start(), calls=%async_computation.1 | async-start | bytes 8912896 | tf_op jit(solution)/shard_map/all_gather | solution.py:42
  7.3 215.0 %reduce-scatter.4.cloned.1.call-start = ((), (), s32[]{:S(2)}) async-start(), calls=%async_computation.2 | async-start | bytes 1081344 | tf_op jit(solution)/shard_map/reduce_scatter | solution.py:44
  8.1 3.9 %collective-permute-start = (bf16[128,128]{1,0:T(8,128)(2,1)S(1)}, bf16[128,128]{1,0:T(8,128)(2,1)S(1)}, u32[]{:S(2)}, u32[]{:S(2)}) collective-permute-start(bf16[128,128]{1,0:T(8,128)(2,1)S(1)} %get-tuple-element.5), channel_id=1, source_target_pairs={{0,16},{16,32},{32,48},{48,64},{64,80},{80,96},{96,112},{112,128},... | collective-permute-start | bytes 98312 | tf_op jit(solution)/shard_map/ppermute | solution.py:15
  9.8 4.8 %collective-permute-start.1 = (bf16[128,128]{1,0:T(8,128)(2,1)S(1)}, bf16[128,128]{1,0:T(8,128)(2,1)S(1)}, u32[]{:S(2)}, u32[]{:S(2)}) collective-permute-start(bf16[128,128]{1,0:T(8,128)(2,1)S(1)} %get-tuple-element.6), channel_id=1, source_target_pairs={{16,0},{32,16},{48,32},{64,48},{80,64},{96,80},{112,96},{128,112},... | collective-permute-start | bytes 98312 | tf_op jit(solution)/shard_map/ppermute | solution.py:18
Sparse Core Ops, SparseCore 0:
  10.3 97.8 all-gather.1
  114.3 107.9 reduce-scatter.3
where the time goes:
time: 229 us
  waiting for transfers between devices  184 us (80%)
  local copies, waits for them, and re-layouts  15.7 us (7%)
  between operations  13.4 us (6%)
  matrix products  11.3 us (5%)
  starting transfers between devices  3.06 us (1%)
    reduce_scatter x1, waiting for transfers between devices, on_device(): lax.psum_scatter(partial_term, 'mesh', scatter_dimension=0, tiled=True)  108 us
    all_gather x1, waiting for transfers between devices, on_device(): gathered = lax.all_gather(snapshots, 'run', axis=1, tiled=True)  72.4 us
    gather x1, local copies, waits for them, and re-layouts, on_device(): blocked[local_cols].reshape(blocks_here, stored_count * BLK, column_count)  13.4 us
    dot_general x1, matrix products, on_device(): jnp.einsum('bim,bmc->bic', mass_blocks, picked, preferred_element_type=jn...  6.61 us
    dot_general x1, matrix products, contract_nodes(): lax.dot_general(left_cols, right_cols, (((0,), (0,)), ((), ())), preferre...  4.66 us
  transfers between devices with their start and end apart: 4, of which 3 were waited for; matrix products, arithmetic and copies ran while one was open for 10% of the time, Pallas kernels for 0%

commit v1 on v0

--- a/solution.py
+++ b/solution.py
@@ -39,7 +39,9 @@
     picked = blocked[local_cols].reshape(blocks_here, stored_count * BLK, column_count)
     weighted = jnp.einsum("bim,bmc->bic", mass_blocks, picked, preferred_element_type=jnp.float32)
     weighted = weighted.astype(jnp.bfloat16).reshape(node_count, column_count)
-    gathered = lax.all_gather(snapshots, "run", axis=1, tiled=True)
+    gathered = jnp.concatenate(
+        lax.all_to_all(jnp.stack([snapshots] * lax.axis_size("run")), "run", 0, 0), axis=1
+    )
     partial_term = contract_nodes(gathered, weighted)
     gram = lax.psum_scatter(partial_term, "mesh", scatter_dimension=0, tiled=True)
     return gram

time: 229 us -> 269 us (1.17)
  waiting for transfers between devices: 184 us -> 210 us
  starting transfers between devices: 3.06 us -> 13.1 us
  local copies, waits for them, and re-layouts: 15.7 us -> 20.5 us
    all_to_all x0 -> x1, waiting for transfers between devices: none -> 90.6 us  [on_device(): lax.all_to_all(jnp.stack([snapshots] * lax.axis_size('run')), 'run', 0, 0)]
    all_gather x1 -> x0, waiting for transfers between devices: 72.4 us -> none  [on_device(): gathered = lax.all_gather(snapshots, 'run', axis=1, tiled=True)]
    all_to_all x0 -> x1, starting transfers between devices: none -> 10.5 us  [on_device(): lax.all_to_all(jnp.stack([snapshots] * lax.axis_size('run')), 'run', 0, 0)]
    reduce_scatter x1, waiting for transfers between devices: 108 us -> 117 us  [on_device(): lax.psum_scatter(partial_term, 'mesh', scatter_dimension=0, tiled=True)]
    another operation x0 -> x1, local copies, waits for them, and re-layouts: none -> 4.32 us  [on_device(): jnp.stack([snapshots] * lax.axis_size('run'))]
  transfers between devices with their start and end apart: 4 -> 4, of which waited for: 3 -> 3; matrix products, arithmetic and copies ran while one was open for 10% -> 7% of each run, Pallas kernels for 0% -> 0%
where the time goes in v1:
time: 269 us
  waiting for transfers between devices  210 us (78%)
  local copies, waits for them, and re-layouts  20.5 us (8%)
  between operations  13.5 us (5%)
  starting transfers between devices  13.1 us (5%)
  matrix products  12.5 us (5%)
    reduce_scatter x1, waiting for transfers between devices, on_device(): lax.psum_scatter(partial_term, 'mesh', scatter_dimension=0, tiled=True)  117 us
    all_to_all x1, waiting for transfers between devices, on_device(): lax.all_to_all(jnp.stack([snapshots] * lax.axis_size('run')), 'run', 0, 0)  90.6 us
    gather x1, local copies, waits for them, and re-layouts, on_device(): blocked[local_cols].reshape(blocks_here, stored_count * BLK, column_count)  13.5 us
    all_to_all x1, starting transfers between devices, on_device(): lax.all_to_all(jnp.stack([snapshots] * lax.axis_size('run')), 'run', 0, 0)  10.5 us
    dot_general x1, matrix products, contract_nodes(): lax.dot_general(left_cols, right_cols, (((0,), (0,)), ((), ())), preferre...  6.29 us
    dot_general x1, matrix products, on_device(): jnp.einsum('bim,bmc->bic', mass_blocks, picked, preferred_element_type=jn...  6.21 us
  transfers between devices with their start and end apart: 4, of which 3 were waited for; matrix products, arithmetic and copies ran while one was open for 7% of the time, Pallas kernels for 0%

profile of v1, /device:TPU:2, one launch (start us, length us, event | category | flops | bytes accessed | tf_op | source)
XLA Modules:
  0.0 269.2 jit_solution(7395607582551731409)
XLA Ops:
  6.5 1.2 copy.9
  7.8 4.3 %stack.2 = bf16[16,2048,128]{1,2,0:T(8,128)(2,1)} broadcast(bf16[2048,128]{0,1:T(8,128)(2,1)S(1)} %copy.9), dimensions={1,2} | broadcast | bytes 8912896 | tf_op jit(solution)/shard_map/stack | solution.py:43
  12.1 0.0 copy-start
  12.1 0.0 copy-start.1
  12.1 10.5 %all-to-all-start = ((bf16[16,2048,128]{1,2,0:T(8,128)(2,1)}), bf16[16,2048,128]{1,2,0:T(8,128)(2,1)}, u32[]{:S(2)}, u32[]{:S(2)}) async-start(bf16[16,2048,128]{1,2,0:T(8,128)(2,1)} %stack.2), calls=%async_computation | async-start | bytes 16777216 | tf_op jit(solution)/shard_map/all_to_all | solution.py:43
  22.6 0.0 reduce-scatter.4.cloned.1.call-start
  22.7 0.0 copy-done
  22.7 1.3 collective-permute-start
  24.0 1.3 collective-permute-start.1
  25.3 0.0 copy-done.1
  25.3 0.1 copy.8
  25.4 0.1 reshape.24
  25.5 0.0 collective-permute-done
  25.5 1.6 collective-permute-done.1
  27.1 13.5 %gather_fusion = bf16[512,64,128]{2,1,0:T(8,128)(2,1)} fusion(bf16[36,64,128]{2,1,0:T(8,128)(2,1)S(1)} %bitcast.15, s32[1024]{0:T(1024)S(1)} %pad_clamp_fusion), kind=kCustom, calls=%fused_computation | custom fusion | bytes 16779264 | tf_op jit(solution)/shard_map/gather | solution.py:39
  40.6 6.2 %convolution_convert_fusion = bf16[32,128,64]{1,2,0:T(8,128)(2,1)S(1)} fusion(bf16[32,64,1024]{2,1,0:T(8,128)(2,1)} %param.5, bf16[32,1024,128]{2,1,0:T(8,128)(2,1)} %bitcast.16), kind=kOutput, calls=%fused_computation.2 | convolution fusion | flops 537133056 | bytes 13107200 | tf_op jit(solution)/shard_map/bim,bmc->bic/dot_general | solution.py:40
  46.8 90.6 %all-to-all-done = bf16[16,2048,128]{1,2,0:T(8,128)(2,1)} async-done(((bf16[16,2048,128]{1,2,0:T(8,128)(2,1)}), bf16[16,2048,128]{1,2,0:T(8,128)(2,1)}, u32[]{:S(2)}, u32[]{:S(2)}) %all-to-all-start) | async-done | bytes 8388640 | tf_op jit(solution)/shard_map/all_to_all | solution.py:43
  137.5 6.3 %convolution_bitcast_fusion = f32[2048,128]{0,1:T(8,128)S(1)} fusion(bf16[2048,128]{1,0:T(8,128)(2,1)S(1)} %bitcast.17, bf16[2048,2048]{0,1:T(8,128)(2,1)} %bitcast.5), kind=kOutput, calls=%fused_computation.1 | convolution fusion | flops 1073741824 | bytes 9961472 | tf_op jit(solution)/shard_map/dot_general | solution.py:24
  143.8 1.3 copy.11
  145.1 0.0 reduce-scatter.4.cloned.1.call-update
  145.1 117.3 %reduce-scatter.4.cloned.1.call-done = f32[64,128]{1,0:T(8,128)} async-done(((f32[2048,128]{1,0:T(8,128)}), f32[64,128]{1,0:T(8,128)}) %reduce-scatter.4.cloned.1.call-update) | async-done | bytes 32784 | tf_op jit(solution)/shard_map/reduce_scatter | solution.py:46
  (4 shorter events, 0.1 us)
Async XLA Ops:
  12.1 10.6 %copy-start = (bf16[2048,128]{1,0:T(8,128)(2,1)S(1)}, bf16[2048,128]{1,0:T(8,128)(2,1)}, u32[]{:S(2)}) copy-start(bf16[2048,128]{1,0:T(8,128)(2,1)} %param.3) | copy-start | bytes 1572868
  12.1 13.2 %copy-start.1 = (s32[32,16]{0,1:T(8,128)S(1)}, s32[32,16]{0,1:T(8,128)}, u32[]{:S(2)}) copy-start(s32[32,16]{0,1:T(8,128)} %param.4) | copy-start | bytes 6148
  12.1 125.4 %all-to-all-start = ((bf16[16,2048,128]{1,2,0:T(8,128)(2,1)}), bf16[16,2048,128]{1,2,0:T(8,128)(2,1)}, u32[]{:S(2)}, u32[]{:S(2)}) async-start(bf16[16,2048,128]{1,2,0:T(8,128)(2,1)} %stack.2), calls=%async_computation | async-start | bytes 16777216 | tf_op jit(solution)/shard_map/all_to_all | solution.py:43
  22.6 239.7 %reduce-scatter.4.cloned.1.call-start = ((), (), s32[]{:S(2)}) async-start(), calls=%async_computation.2 | async-start | bytes 1081344 | tf_op jit(solution)/shard_map/reduce_scatter | solution.py:46
  22.7 2.8 %collective-permute-start = (bf16[128,128]{1,0:T(8,128)(2,1)S(1)}, bf16[128,128]{1,0:T(8,128)(2,1)S(1)}, u32[]{:S(2)}, u32[]{:S(2)}) collective-permute-start(bf16[128,128]{1,0:T(8,128)(2,1)S(1)} %get-tuple-element.5), channel_id=1, source_target_pairs={{0,16},{16,32},{32,48},{48,64},{64,80},{80,96},{96,112},{112,128},... | collective-permute-start | bytes 98312 | tf_op jit(solution)/shard_map/ppermute | solution.py:15
  24.0 3.1 %collective-permute-start.1 = (bf16[128,128]{1,0:T(8,128)(2,1)S(1)}, bf16[128,128]{1,0:T(8,128)(2,1)S(1)}, u32[]{:S(2)}, u32[]{:S(2)}) collective-permute-start(bf16[128,128]{1,0:T(8,128)(2,1)S(1)} %get-tuple-element.6), channel_id=1, source_target_pairs={{16,0},{32,16},{48,32},{64,48},{80,64},{96,80},{112,96},{128,112},... | collective-permute-start | bytes 98312 | tf_op jit(solution)/shard_map/ppermute | solution.py:18
Sparse Core Ops, SparseCore 0:
  145.2 117.0 reduce-scatter.3
